TPU v7x, 32 devices: a whole 2x2x4 slice. The times are simulated.
32 devices in a mesh: seq: 8 (over z, x), rows: 4 (over y, core).
Axes of the slice: x: 2, y: 2, z: 4, core: 2. Of those that a mesh axis runs over, the one named last changes fastest.
Arguments:
- activations: float32 [8, 2048, 512], P('rows', 'seq'), may hold values from -6 to 6
- cotangent: float32 [8, 2048, 512], P('rows', 'seq')
- seq_starts: int32 [8, 3], P('rows'), may hold values from 0 to 2048, as said below
- attn_weight: float32 [4, 512, 512], P(None, 'rows')
- up_weight: float32 [512, 2048], P('rows'), may hold values from -0.25 to 0.25
- down_weight: float32 [2048, 512], P('rows'), may hold values from -0.125 to 0.125
- vectors: float32 [9, 512], replicated
- attn_m: float32 [4, 512, 512], P(None, 'rows'), may hold values from -0.0022552744 to 0.0022552744
- up_m: float32 [512, 2048], P('rows'), may hold values from -0.0022552744 to 0.0022552744
- down_m: float32 [2048, 512], P('rows'), may hold values from -0.0022552744 to 0.0022552744
- vec_m: float32 [9, 512], replicated, may hold values from -0.004510549 to 0.004510549
- attn_v: float32 [4, 512, 512], P(None, 'rows'), may hold values from 3.1789145e-07 to 1.2715658e-06
- up_v: float32 [512, 2048], P('rows'), may hold values from 3.1789145e-07 to 1.2715658e-06
- down_v: float32 [2048, 512], P('rows'), may hold values from 3.1789145e-07 to 1.2715658e-06
- vec_v: float32 [9, 512], replicated, may hold values from 1.2715658e-06 to 5.086263e-06
Outputs:
- out_act: float32 [8, 2048, 512], P('rows', 'seq')
- in_grad: float32 [8, 2048, 512], P('rows', 'seq')
- grad_norm: float32 [], replicated
- attn_grad: float32 [4, 512, 512], P(None, 'rows')
- up_grad: float32 [512, 2048], P('rows')
- down_grad: float32 [2048, 512], P('rows')
- vec_grad: float32 [9, 512], replicated
- attn_new: float32 [4, 512, 512], P(None, 'rows')
- up_new: float32 [512, 2048], P('rows')
- down_new: float32 [2048, 512], P('rows')
- vec_new: float32 [9, 512], replicated
- attn_m_new: float32 [4, 512, 512], P(None, 'rows')
- up_m_new: float32 [512, 2048], P('rows')
- down_m_new: float32 [2048, 512], P('rows')
- vec_m_new: float32 [9, 512], replicated
- attn_v_new: float32 [4, 512, 512], P(None, 'rows')
- up_v_new: float32 [512, 2048], P('rows')
- down_v_new: float32 [2048, 512], P('rows')
- vec_v_new: float32 [9, 512], replicated
Inputs may be any that keep to these rules, and one draw needn't show every extreme that they name: `seq_starts`: in each row the entries rise from 0; an entry equal to 2048 marks an unused slot and all after it are unused. Of the 2 rows that share one index of rows, at least one holds a single sequence over the whole row.
All inputs are finite; a program needn't handle non-finite values.
Results may differ from a plain program's by a relative error of at most 0.0003.
Values sent between devices are 32-bit elements; how exact they have to be, the bound alone decides.
No kernel may reach another device: no remote copies, remote signals or barrier semaphores. Data moves between devices by JAX's collectives and lax.ppermute only.
A program may use at most 192 MiB of HBM per device.

v0:
```python
import jax
import jax.numpy as jnp
from jax import lax
from jax.sharding import PartitionSpec as P

HEADS = 8
HEAD_DIM = 64
STEP = 5


EPS_NORM = 1e-05
EPS_DEN = 1e-06
CLIP_AT = 1.0
BETA_ONE = 0.5
BETA_TWO = 0.5
RATE_MAT = 0.02
RATE_VEC = 0.1
DECAY_MAT = 0.1
EPS_ADAM = 1e-08
PRECISE = lax.Precision.HIGHEST


def entering(part, axis, combine, identity, reverse):
    count = lax.axis_size(axis)
    place = lax.axis_index(axis)
    ahead = count - 1 - place if reverse else place
    gathered = jax.tree.map(lambda a: lax.all_gather(a, axis), part)
    state = jax.tree.map(lambda a, e: jnp.zeros_like(a) + jnp.asarray(e, a.dtype), part, identity)

    def one(hop, state):
        source = count - 1 - hop if reverse else hop
        return combine(
            state, jax.tree.map(lambda a: lax.dynamic_index_in_dim(a, source, 0, False), gathered)
        )

    return lax.fori_loop(0, ahead, one, state)


def feature(value):
    return jax.nn.elu(value) + 1.0


def layer_norm(inputs, scale_gain, offset):
    average = jnp.mean(inputs, axis=-1, keepdims=True)
    centred = inputs - average
    spread = jnp.mean(centred * centred, axis=-1, keepdims=True)
    return centred * lax.rsqrt(spread + EPS_NORM) * scale_gain + offset


def chain_join(earlier, later):
    flag_early, state_early, sum_early = earlier
    flag_late, state_late, sum_late = later
    passing = 1.0 - flag_late
    return (
        jnp.maximum(flag_early, flag_late),
        state_late + passing[:, None, None, None] * state_early,
        sum_late + passing[:, None, None] * sum_early,
    )


def adamw_step(weight, gradient, first_m, second_m, factor, rate, decay):
    clipped = gradient * factor
    new_m = BETA_ONE * first_m + (1.0 - BETA_ONE) * clipped
    new_v = BETA_TWO * second_m + (1.0 - BETA_TWO) * clipped * clipped
    moved = new_m / (1.0 - BETA_ONE**STEP) / (jnp.sqrt(new_v / (1.0 - BETA_TWO**STEP)) + EPS_ADAM)
    return (clipped, weight - rate * (moved + decay * weight), new_m, new_v)


def body(
    activations,
    cotangent,
    seq_starts,
    attn_weight,
    up_weight,
    down_weight,
    vectors,
    attn_m,
    up_m,
    down_m,
    vec_m,
    attn_v,
    up_v,
    down_v,
    vec_v,
):
    attention_full, up_full, down_full = (
        lax.all_gather(attn_weight, "rows", axis=1, tiled=True),
        lax.all_gather(up_weight, "rows", axis=0, tiled=True),
        lax.all_gather(down_weight, "rows", axis=0, tiled=True),
    )
    row_count, length, width = activations.shape
    hidden_width = up_full.shape[1]
    stretch_start = lax.axis_index("seq") * length
    token_positions = stretch_start + jnp.arange(length, dtype=jnp.int32)
    doc_ids = jnp.sum(
        (seq_starts[:, None, :] <= token_positions[None, :, None]).astype(jnp.int32), axis=2
    )
    prev_doc = jnp.sum((seq_starts <= stretch_start - 1).astype(jnp.int32), axis=1)
    last_doc = doc_ids[:, -1]
    reset_flag = (last_doc != prev_doc).astype(jnp.float32)
    kept_last = (doc_ids == last_doc[:, None]).astype(jnp.float32)[:, :, None, None]
    use_state = (doc_ids == prev_doc[:, None]).astype(jnp.float32)[:, :, None]
    causal = token_positions[:, None] >= token_positions[None, :]
    doc_mask = ((doc_ids[:, :, None] == doc_ids[:, None, :]) & causal[None]).astype(jnp.float32)

    def project(inputs, attention, vector_set):
        normed = layer_norm(inputs, vector_set[0], vector_set[1]).reshape(row_count * length, width)

        def head_split(matrix):
            return jnp.dot(normed, matrix, precision=PRECISE).reshape(
                row_count, length, HEADS, HEAD_DIM
            )

        return (
            feature(head_split(attention[0])),
            feature(head_split(attention[1])),
            head_split(attention[2]),
        )

    def summarize(feat_k, values_v):
        masked = feat_k * kept_last
        return (
            jnp.einsum("rshe,rshf->rhef", masked, values_v, precision=PRECISE),
            jnp.sum(masked, axis=1),
        )

    def finish(
        inputs,
        feat_q,
        feat_k,
        values_v,
        out_matrix,
        up_matrix,
        down_matrix,
        vector_set,
        state_in,
        sum_in,
    ):
        scores = (
            jnp.einsum("rthe,rshe->rhts", feat_q, feat_k, precision=PRECISE) * doc_mask[:, None]
        )
        numer = jnp.einsum("rhts,rshe->rthe", scores, values_v, precision=PRECISE)
        denom = jnp.transpose(jnp.sum(scores, axis=3), (0, 2, 1))
        numer = numer + use_state[..., None] * jnp.einsum(
            "rthe,rhef->rthf", feat_q, state_in, precision=PRECISE
        )
        denom = denom + use_state * jnp.einsum("rthe,rhe->rth", feat_q, sum_in, precision=PRECISE)
        mixed = (numer / (denom[..., None] + EPS_DEN)).reshape(row_count * length, width)
        flat = inputs.reshape(row_count * length, width)
        resid = flat + jnp.dot(mixed, out_matrix, precision=PRECISE)
        second = layer_norm(resid, vector_set[2], vector_set[3])
        upped = jnp.dot(second, up_matrix, precision=PRECISE) + vector_set[5:].reshape(hidden_width)
        result = (
            resid
            + jnp.dot(jax.nn.gelu(upped, approximate=False), down_matrix, precision=PRECISE)
            + vector_set[4]
        )
        return result.reshape(row_count, length, width)

    feat_q, feat_k, values_v = project(activations, attention_full, vectors)
    (state_local, sum_local), summary_back = jax.vjp(summarize, feat_k, values_v)
    nothing = (jnp.zeros_like(reset_flag), jnp.zeros_like(state_local), jnp.zeros_like(sum_local))
    _, state_in, sum_in = entering(
        (reset_flag, state_local, sum_local), "seq", chain_join, nothing, False
    )
    out_act, finish_back = jax.vjp(
        finish,
        activations,
        feat_q,
        feat_k,
        values_v,
        attention_full[3],
        up_full,
        down_full,
        vectors,
        state_in,
        sum_in,
    )
    (
        grad_x_late,
        grad_q,
        grad_k,
        grad_v,
        grad_out,
        grad_up,
        grad_down,
        grad_vec_late,
        grad_state,
        grad_sum,
    ) = finish_back(cotangent)
    _, later_state, later_sum = entering(
        (reset_flag, grad_state, grad_sum), "seq", chain_join, nothing, True
    )
    extra_k, extra_v = summary_back((later_state, later_sum))
    cotangents = (grad_q, grad_k + extra_k, grad_v + extra_v)
    _, project_again = jax.vjp(project, activations, attention_full, vectors)
    grad_x_early, grad_attn_early, grad_vec_early = project_again(cotangents)
    in_grad = grad_x_late + grad_x_early
    grad_attn = jnp.concatenate([grad_attn_early[:3], grad_out[None]], axis=0)
    grad_vec = grad_vec_late + grad_vec_early
    row_rank = lax.axis_index("rows")
    groups = lax.axis_size("rows")
    total_attn, total_up, total_down, total_vec = lax.psum(
        (grad_attn, grad_up, grad_down, grad_vec), ("seq", "rows")
    )
    square = (
        jnp.sum(total_attn * total_attn)
        + jnp.sum(total_up * total_up)
        + jnp.sum(total_down * total_down)
        + jnp.sum(total_vec * total_vec)
    )
    rows_width = width // groups
    rows_hidden = hidden_width // groups
    shard_attn = lax.dynamic_slice_in_dim(total_attn, row_rank * rows_width, rows_width, 1)
    shard_up = lax.dynamic_slice_in_dim(total_up, row_rank * rows_width, rows_width, 0)
    shard_down = lax.dynamic_slice_in_dim(total_down, row_rank * rows_hidden, rows_hidden, 0)
    grad_norm = jnp.sqrt(square)
    factor = jnp.minimum(1.0, CLIP_AT / (grad_norm + 1e-06))
    attn_g, attn_new, attn_m_new, attn_v_new = adamw_step(
        attn_weight, shard_attn, attn_m, attn_v, factor, RATE_MAT, DECAY_MAT
    )
    up_g, up_new, up_m_new, up_v_new = adamw_step(
        up_weight, shard_up, up_m, up_v, factor, RATE_MAT, DECAY_MAT
    )
    down_g, down_new, down_m_new, down_v_new = adamw_step(
        down_weight, shard_down, down_m, down_v, factor, RATE_MAT, DECAY_MAT
    )
    vec_g, vec_new, vec_m_new, vec_v_new = adamw_step(
        vectors, total_vec, vec_m, vec_v, factor, RATE_VEC, 0.0
    )
    return (
        out_act,
        in_grad,
        grad_norm,
        attn_g,
        up_g,
        down_g,
        vec_g,
        attn_new,
        up_new,
        down_new,
        vec_new,
        attn_m_new,
        up_m_new,
        down_m_new,
        vec_m_new,
        attn_v_new,
        up_v_new,
        down_v_new,
        vec_v_new,
    )


def solution(mesh):
    in_specs = (
        P("rows", "seq", None),
        P("rows", "seq", None),
        P("rows", None),
        P(None, "rows", None),
        P("rows", None),
        P("rows", None),
        P(),
        P(None, "rows", None),
        P("rows", None),
        P("rows", None),
        P(),
        P(None, "rows", None),
        P("rows", None),
        P("rows", None),
        P(),
    )
    out_specs = (
        P("rows", "seq", None),
        P("rows", "seq", None),
        P(),
        P(None, "rows", None),
        P("rows", None),
        P("rows", None),
        P(),
        P(None, "rows", None),
        P("rows", None),
        P("rows", None),
        P(),
        P(None, "rows", None),
        P("rows", None),
        P("rows", None),
        P(),
        P(None, "rows", None),
        P("rows", None),
        P("rows", None),
        P(),
    )
    return jax.shard_map(body, mesh=mesh, in_specs=in_specs, out_specs=out_specs, check_vma=False)
```

profile of v0, /device:TPU:0, one launch (start us, length us, event | category | flops | bytes accessed | tf_op | source)
XLA Modules:
  0.0 620.6 jit_solution(9694726002119822886)
XLA Ops:
  15.2 31.6 %all-gather.11.cloned.1.call-done = f32[4,512,512]{2,1,0:T(8,128)} async-done(((f32[4,128,512]{2,1,0:T(8,128)}), f32[4,512,512]{2,1,0:T(8,128)}) %all-gather.11.cloned.1.call-update) | async-done | bytes 4194320 | tf_op jit(solution)/shard_map/all_gather | solution.py:87
  46.8 3.9 fusion.137
  62.8 20.6 %all-gather.4 = f32[8,1,2]{2,1,0:T(1,128)S(1)} all-gather(f32[1,1,2]{2,1,0:T(1,128)S(1)} %fusion.112), channel_id=1, replica_groups=mesh['seq'=8,'rows'=4] {'seq'}, dimensions={0}, use_global_device_ids=true | all-gather | bytes 72 | tf_op jit(solution)/shard_map/all_gather | solution.py:27
  88.5 31.4 %all-gather.1 = f32[16,8,64]{2,1,0:T(8,128)S(1)} all-gather(f32[2,8,64]{2,1,0:T(8,128)S(1)} %multiply_reduce_fusion.11), channel_id=3, replica_groups=mesh['seq'=8,'rows'=4] {'seq'}, dimensions={0}, use_global_device_ids=true | all-gather | bytes 36864 | tf_op jit(solution)/shard_map/all_gather | solution.py:27
  124.0 5.9 multiply_reduce_fusion.3
  129.9 5.9 all-gather.17.cloned.1.call-done
  150.3 19.9 %all-gather.13.cloned.1.call-done = f32[512,2048]{1,0:T(8,128)} async-done(((f32[128,2048]{1,0:T(8,128)}), f32[512,2048]{1,0:T(8,128)}) %all-gather.13.cloned.1.call-update) | async-done | bytes 4194320 | tf_op jit(solution)/shard_map/all_gather | solution.py:88
  170.2 10.8 %fusion.85 = f32[512,2048]{1,0:T(8,128)} fusion(f32[512,2048]{1,0:T(8,128)} %all-gather.13.cloned.1.call-done, f32[512,512]{1,0:T(8,128)S(1)} %get-tuple-element.344, f32[512]{0:T(512)S(1)} %bitcast.258, f32[512]{0:T(512)S(1)} %bitcast.254, f32[512]{0:T(512)S(1)} %fusion.109, f32[512]{0:T(512)S(1)} %broadcast_multiply_fusion.2), kind=kOutput, calls=%fused_computation.147 | convolution fusion | flops 6443499520 | bytes 9445376 | tf_op jit(solution)/shard_map/jvp()/dot_general | solution.py:152
  181.0 25.1 %all-gather.15.cloned.1.call-done = f32[2048,512]{1,0:T(8,128)} async-done(((f32[512,512]{1,0:T(8,128)}), f32[2048,512]{1,0:T(8,128)}) %all-gather.15.cloned.1.call-update) | async-done | bytes 4194320 | tf_op jit(solution)/shard_map/all_gather | solution.py:89
  206.1 19.9 %fusion.133 = (f32[2048]{0:T(1024)S(1)}, f32[512,2048]{1,0:T(8,128)S(1)}, f32[512,2048]{1,0:T(8,128)}) fusion(f32[512,2048]{1,0:T(8,128)} %fusion.85, f32[2048]{0:T(1024)S(1)} %bitcast.260, f32[512,512]{1,0:T(8,128)} %bitcast.231, f32[2048,512]{1,0:T(8,128)} %all-gather.15.cloned.1.call-done), kind=kOutput, calls=%fused_computation.210 | convolution fusion | flops 6518994944 | bytes 17842176 | tf_op jit(solution)/shard_map/transpose(jvp())/dot_general | solution.py:155
  226.1 7.2 %multiply_reduce_fusion.5 = (f32[512]{0:T(512)S(1)}, f32[512]{0:T(512)S(1)}, f32[512]{0:T(512)S(1)}, f32[512,512]{1,0:T(8,128)S(1)}) fusion(f32[512,512]{1,0:T(8,128)S(1)} %get-tuple-element.344, f32[512]{0:T(512)S(1)} %fusion.109, f32[512]{0:T(512)S(1)} %broadcast_multiply_fusion.2, f32[512]{0:T(512)S(1)} %bitcast.255, ...), kind=kOutput, calls=%fused_computation.122 | convolution fusion | flops 6444546560 | bytes 10498048 | tf_op jit(solution)/shard_map/transpose(jvp())/dot_general | solution.py:152
  253.3 31.5 %all-gather.3 = f32[16,8,64]{2,1,0:T(8,128)S(1)} all-gather(f32[2,8,64]{2,1,0:T(8,128)S(1)} %bitcast.271), channel_id=5, replica_groups=mesh['seq'=8,'rows'=4] {'seq'}, dimensions={0}, use_global_device_ids=true | all-gather | bytes 36864 | tf_op jit(solution)/shard_map/all_gather | solution.py:27
  287.6 4.4 convolution_bitcast_fusion.1
  292.1 8.8 %fusion.84 = f32[512,2048]{1,0:T(8,128)} fusion(f32[512,2048]{1,0:T(8,128)S(1)} %copy-done.7, f32[512,512]{1,0:T(8,128)S(1)} %get-tuple-element.344, f32[512]{0:T(512)S(1)} %bitcast.259, f32[512]{0:T(512)S(1)} %bitcast.257, f32[512]{0:T(512)S(1)} %fusion.109, f32[512]{0:T(512)S(1)} %broadcast_multiply_fusion.2), kind=kOutput, calls=%fused_computation.146 | convolution fusion | flops 6443499520 | bytes 9445376 | tf_op jit(solution)/shard_map/transpose(jvp())/dot_general | solution.py:152
  300.9 8.5 %fusion.40 = f32[2048,512]{1,0:T(8,128)} fusion(f32[512,512]{1,0:T(8,128)S(1)} %bitcast.232, f32[512,2048]{1,0:T(8,128)S(1)} %copy-done.4, f32[512,2048]{1,0:T(8,128)S(1)} %copy-done, f32[2048]{0:T(1024)S(1)} %bitcast.261), kind=kOutput, calls=%fused_computation.75 | convolution fusion | flops 6445596672 | bytes 13639680 | tf_op jit(solution)/shard_map/transpose(jvp())/dot_general | solution.py:155
  309.4 5.0 all-gather.19.cloned.1.call-done
  315.3 15.6 %while.31 = (s32[]{:T(128)}, f32[2,8,64,64]{3,2,1,0:T(8,128)}, f32[2,8,64]{2,1,0:T(8,128)S(1)}, s32[]{:T(128)}, f32[8,2,8,64,64]{4,3,2,1,0:T(8,128)}, /*index=5*...) while((s32[]{:T(128)}, f32[2,8,64,64]{3,2,1,0:T(8,128)}, ...), condition=%wide.region_14.15_spmd, body=%wide.region_13.14_spmd.sunk | while | flops 133128 | bytes 798927 | solution.py:36
  333.8 6.8 %fusion.31 = f32[2,256,8,64]{1,3,2,0:T(8,128)S(1)} fusion(f32[2,8,64,256]{3,2,1,0:T(8,128)S(1)} %fusion.80, f32[2,8,256,256]{2,3,1,0:T(8,128)} %get-tuple-element.340, f32[2,256,256]{1,2,0:T(8,128)} %copy-done.31, f32[2,256,8,64]{1,3,2,0:T(8,128)} %copy-done.27, f32[2,8,256]{2,1,0:T(8,128)S(1)} %get-tuple-element.321), kind=kOutput, calls=%fused_computation.58 | convolution fusion | flops 806879232 | bytes 7880704 | tf_op jit(solution)/shard_map/transpose(jvp(rhts,rshe->rthe))/dot_general | solution.py:142
  343.9 4.9 fusion.53
  361.1 13.4 %fusion.43 = f32[512,512]{1,0:T(8,128)} fusion(f32[512,512]{1,0:T(8,128)S(1)} %get-tuple-element.344, f32[2048,512]{1,0:T(8,128)} %all-gather.15.cloned.1.call-done, f32[512,2048]{1,0:T(8,128)} %get-tuple-element.319, f32[512,2048]{1,0:T(8,128)} %fusion.85, f32[2048]{0:T(1024)S(1)} %bitcast.262, f32[512]{0:T(512)S(1)} %bitcast.267), kind=kOutput, calls=%fused_computation.78 | convolution fusion | flops 6446120960 | bytes 14690304 | tf_op jit(solution)/shard_map/jvp()/dot_general | solution.py:155
  386.1 38.9 %psum.31 = f32[9,512]{1,0:T(8,128)S(1)} all-reduce(f32[9,512]{1,0:T(8,128)S(1)} %add_add_fusion.4), channel_id=1, replica_groups=mesh['seq'=8,'rows'=4] {'seq','rows'}, use_global_device_ids=true, to_apply=%region_29.30 | all-reduce | flops 4608 | bytes 36864 | tf_op jit(solution)/shard_map/psum | solution.py:203
  426.9 163.2 %all-reduce.12.cloned.1.call-done = (f32[4,512,512]{2,1,0:T(8,128)}, f32[512,2048]{1,0:T(8,128)}, f32[2048,512]{1,0:T(8,128)}) async-done(((f32[4,512,512]{2,1,0:T(8,128)}, f32[512,2048]{1,0:T(8,128)}, f32[2048,512]{1,0:T(8,128)}), (f32[4,512,512]{2,1,0:T(8,128)}, f32[512,2048]{1,0:T(8,128)}, f32[2048,512]{1,0:T(8,128)})) %all-reduce.12.cloned.1.call-update) | async-done | bytes 12582928 | tf_op jit(solution)/shard_map/psum | solution.py:203
  590.1 4.0 multiply_reduce_fusion.2
  600.2 4.1 multiply_subtract_fusion.2
  (236 shorter events, 125.5 us)
Async XLA Ops:
  7.2 39.6 %all-gather.11.cloned.1.call-start = ((), (), s32[]{:S(2)}) async-start(), calls=%async_computation | async-start | bytes 5242880 | tf_op jit(solution)/shard_map/all_gather | solution.py:87
  7.9 127.9 %all-gather.17.cloned.1.call-start = ((), (), s32[]{:S(2)}) async-start(), calls=%async_computation.3 | async-start | bytes 4718592 | tf_op jit(solution)/shard_map/all_gather | solution.py:27
  59.0 82.1 %copy-start.8 = (f32[2,256,8,64]{1,3,2,0:T(8,128)}, f32[2,256,8,64]{1,3,2,0:T(8,128)S(1)}, u32[]{:S(2)}) copy-start(f32[2,256,8,64]{1,3,2,0:T(8,128)S(1)} %fusion.70) | copy-start | bytes 3145732
  61.4 108.8 %all-gather.13.cloned.1.call-start = ((), (), s32[]{:S(2)}) async-start(), calls=%async_computation.1 | async-start | bytes 5242880 | tf_op jit(solution)/shard_map/all_gather | solution.py:88
  62.1 144.0 %all-gather.15.cloned.1.call-start = ((), (), s32[]{:S(2)}) async-start(), calls=%async_computation.2 | async-start | bytes 5242880 | tf_op jit(solution)/shard_map/all_gather | solution.py:89
  62.7 251.7 %all-gather.19.cloned.1.call-start = ((), (), s32[]{:S(2)}) async-start(), calls=%async_computation.4 | async-start | bytes 4718592 | tf_op jit(solution)/shard_map/all_gather | solution.py:27
  83.9 57.3 %copy-start.31 = (f32[2,256,256]{1,2,0:T(8,128)}, f32[2,256,256]{1,2,0:T(8,128)S(1)}, u32[]{:S(2)}) copy-start(f32[2,256,256]{1,2,0:T(8,128)S(1)} %and_convert_fusion.2) | copy-start | bytes 1572868
  86.6 37.4 %copy-start.38 = (f32[2,256,8,64]{1,3,2,0:T(8,128)S(1)}, f32[2,256,8,64]{1,3,2,0:T(8,128)}, u32[]{:S(2)}) copy-start(f32[2,256,8,64]{1,3,2,0:T(8,128)} %copy-done.37) | copy-start | bytes 3145732
  206.1 20.0 %copy-start.5 = (f32[512,2048]{1,0:T(8,128)S(1)}, f32[512,2048]{1,0:T(8,128)}, u32[]{:S(2)}) copy-start(f32[512,2048]{1,0:T(8,128)} %all-gather.13.cloned.1.call-done) | copy-start | bytes 12582916
  240.3 349.7 %all-reduce.12.cloned.1.call-start = ((), (), s32[]{:S(2)}) async-start(), calls=%async_computation.5 | async-start | bytes 25165824 | tf_op jit(solution)/shard_map/psum | solution.py:203
  251.0 33.8 %copy-start.14 = (f32[512,512]{1,0:T(8,128)S(1)}, f32[512,512]{1,0:T(8,128)}, u32[]{:S(2)}) copy-start(f32[512,512]{1,0:T(8,128)} %copy-done.13) | copy-start | bytes 3145732
  251.0 33.8 %copy-start.24 = (f32[64,8,2,256]{3,1,2,0:T(8,128)S(1)}, f32[64,8,2,256]{3,1,2,0:T(8,128)}, u32[]{:S(2)}) copy-start(f32[64,8,2,256]{3,1,2,0:T(8,128)} %copy-done.23) | copy-start | bytes 3145732
  251.9 35.7 %copy-start.21 = (f32[64,8,2,256]{3,1,2,0:T(8,128)}, f32[64,8,2,256]{3,1,2,0:T(8,128)S(1)}, u32[]{:S(2)}) copy-start(f32[64,8,2,256]{3,1,2,0:T(8,128)S(1)} %copy.152) | copy-start | bytes 3145732
  252.0 40.1 %copy-start.7 = (f32[512,2048]{1,0:T(8,128)S(1)}, f32[512,2048]{1,0:T(8,128)}, u32[]{:S(2)}) copy-start(f32[512,2048]{1,0:T(8,128)} %copy-done.6) | copy-start | bytes 12582916
  292.1 8.8 %copy-start = (f32[512,2048]{1,0:T(8,128)S(1)}, f32[512,2048]{1,0:T(8,128)}, u32[]{:S(2)}) copy-start(f32[512,2048]{1,0:T(8,128)} %fusion.85) | copy-start | bytes 12582916
  292.1 8.8 %copy-start.4 = (f32[512,2048]{1,0:T(8,128)S(1)}, f32[512,2048]{1,0:T(8,128)}, u32[]{:S(2)}) copy-start(f32[512,2048]{1,0:T(8,128)} %get-tuple-element.319) | copy-start | bytes 12582916
  292.1 8.8 %copy-start.19 = (f32[2,256,512]{2,1,0:T(8,128)S(1)}, f32[2,256,512]{2,1,0:T(8,128)}, u32[]{:S(2)}) copy-start(f32[2,256,512]{2,1,0:T(8,128)} %param.20) | copy-start | bytes 3145732
  333.8 7.7 %copy-start.2 = (f32[2,8,64,64]{3,2,1,0:T(8,128)S(1)}, f32[2,8,64,64]{3,2,1,0:T(8,128)}, u32[]{:S(2)}) copy-start(f32[2,8,64,64]{3,2,1,0:T(8,128)} %get-tuple-element.193) | copy-start | bytes 786436
  333.8 7.7 %copy-start.10 = (f32[2,256,8,64]{1,3,2,0:T(8,128)S(1)}, f32[2,256,8,64]{1,3,2,0:T(8,128)}, u32[]{:S(2)}) copy-start(f32[2,256,8,64]{1,3,2,0:T(8,128)} %copy-done.8) | copy-start | bytes 3145732
  341.5 11.9 %copy-start.16 = (f32[64,8,2,256]{3,1,2,0:T(8,128)}, f32[64,8,2,256]{3,1,2,0:T(8,128)S(1)}, u32[]{:S(2)}) copy-start(f32[64,8,2,256]{3,1,2,0:T(8,128)S(1)} %copy.150) | copy-start | bytes 3145732
  361.1 13.4 %copy-start.11 = (f32[4,512,512]{2,1,0:T(8,128)S(1)}, f32[4,512,512]{2,1,0:T(8,128)}, u32[]{:S(2)}) copy-start(f32[4,512,512]{2,1,0:T(8,128)} %all-gather.11.cloned.1.call-done) | copy-start | bytes 12582916
  361.1 13.4 %copy-start.17 = (f32[64,8,2,256]{3,1,2,0:T(8,128)S(1)}, f32[64,8,2,256]{3,1,2,0:T(8,128)}, u32[]{:S(2)}) copy-start(f32[64,8,2,256]{3,1,2,0:T(8,128)} %copy-done.16) | copy-start | bytes 3145732
  361.1 16.9 %copy-start.26 = (f32[64,8,2,256]{3,1,2,0:T(8,128)S(1)}, f32[64,8,2,256]{3,1,2,0:T(8,128)}, u32[]{:S(2)}) copy-start(f32[64,8,2,256]{3,1,2,0:T(8,128)} %copy-done.25) | copy-start | bytes 3145732
  381.7 43.9 %copy-start.15 = (f32[512,512]{1,0:T(8,128)S(1)}, f32[512,512]{1,0:T(8,128)}, u32[]{:S(2)}) copy-start(f32[512,512]{1,0:T(8,128)} %copy-done.13) | copy-start | bytes 3145732
  (41 other events, 162.2 us)
Sparse Core Ops, SparseCore 0:
  9.6 37.1 all-gather.10
  61.5 74.2 all-gather.16
  137.4 32.7 all-gather.12
  171.6 34.5 all-gather.14
  240.5 73.9 all-gather.18
  359.9 230.0 all-reduce.11
where the time goes:
time: 628 us; the launch traced here: 621 us
  waiting for transfers between devices  253 us (40%)
  matrix products  154 us (25%)
  blocking collectives  122 us (19%)
  other arithmetic  49 us (8%)
  local copies, waits for them, and re-layouts  22.8 us (4%)
  between operations  19.1 us (3%)
    psum x1, waiting for transfers between devices, body(): lax.psum((grad_attn, grad_up, grad_down, grad_vec), ('seq', 'rows'))  163 us
    all_gather x3, blocking collectives, entering(): gathered = jax.tree.map(lambda a: lax.all_gather(a, axis), part)  83.5 us
    dot_general x3, matrix products, finish(): jnp.dot(jax.nn.gelu(upped, approximate=False), down_matrix, precision=PRE...  41.9 us
    psum x1, blocking collectives, body(): lax.psum((grad_attn, grad_up, grad_down, grad_vec), ('seq', 'rows'))  38.9 us
    all_gather x1, waiting for transfers between devices, body(): lax.all_gather(attn_weight, 'rows', axis=1, tiled=True)  31.6 us
    dot_general x9, matrix products, head_split(): jnp.dot(normed, matrix, precision=PRECISE)  30.5 us
    dot_general x3, matrix products, finish(): jnp.dot(second, up_matrix, precision=PRECISE)  26.8 us
    all_gather x1, waiting for transfers between devices, body(): lax.all_gather(down_weight, 'rows', axis=0, tiled=True)  25.1 us
  transfers between devices with their start and end apart: 6, of which 6 were waited for; matrix products, arithmetic and copies ran while one was open for 18% of the time, Pallas kernels for 0%

commit v1 on v0

v1 whole, which is shorter than its diff:
```python
import functools
import math

import jax
import jax.numpy as jnp
from jax import lax
from jax.experimental import pallas as pl
from jax.experimental.pallas import tpu as pltpu
from jax.sharding import PartitionSpec as P

HEADS = 8
HEAD_DIM = 64
PAIRS = HEADS // 2
LANES = 2 * HEAD_DIM
STEP = 5

EPS_NORM = 1e-05
EPS_DEN = 1e-06
CLIP_AT = 1.0
BETA_ONE = 0.5
BETA_TWO = 0.5
RATE_MAT = 0.02
RATE_VEC = 0.1
DECAY_MAT = 0.1
EPS_ADAM = 1e-08

F32 = jnp.float32
BF16 = jnp.bfloat16
VMEM = pl.BlockSpec(memory_space=pltpu.VMEM)
SMEM = pl.BlockSpec(memory_space=pltpu.SMEM)
LIMIT = 56 * 1024 * 1024


def split(a):
    high = a.astype(BF16)
    return high, (a - high.astype(F32)).astype(BF16)


def dot3(a, b, ca=1, cb=0):
    dims = (((ca,), (cb,)), ((), ()))

    def one(p, q):
        return lax.dot_general(p, q, dims, preferred_element_type=F32)

    return one(a[0], b[0]) + (one(a[0], b[1]) + one(a[1], b[0]))


def dot2(a, b):
    dims = (((1,), (0,)), ((), ()))
    return sum(lax.dot_general(p, b, dims, preferred_element_type=F32) for p in a)


def phi(u):
    return jnp.where(u > 0, u + 1.0, jnp.exp(jnp.minimum(u, 0.0)))


def normalise(x):
    centred = x - jnp.mean(x, axis=1, keepdims=True)
    scale = lax.rsqrt(jnp.mean(centred * centred, axis=1, keepdims=True) + EPS_NORM)
    return centred * scale, scale


def normalise_back(grad, unit, scale):
    inner = jnp.mean(grad * unit, axis=1, keepdims=True)
    return scale * (grad - jnp.mean(grad, axis=1, keepdims=True) - unit * inner)


def first_head(shape):
    return lax.broadcasted_iota(jnp.int32, shape, len(shape) - 1) % LANES < HEAD_DIM


def pick(value, head):
    return jnp.where(first_head(value.shape) == (head == 0), value, 0.0)


def block_ones():
    shape = (LANES, LANES)
    rows, lanes = (lax.broadcasted_iota(jnp.int32, shape, d) // HEAD_DIM for d in (0, 1))
    return jnp.where(rows == lanes, 1.0, 0.0).astype(BF16)


class Info:
    def __init__(self, ref, length, slots):
        self.ref, self.length, self.slots = ref, length, slots
        self.me, self.place, self.first = ref[0], ref[1], ref[2]

    def starts(self, r):
        return [self.ref[3 + r * self.slots + i] for i in range(self.slots)]

    def causal(self, r, flipped=False):
        shape = (self.length, self.length)
        t = self.first + lax.broadcasted_iota(jnp.int32, shape, 1 if flipped else 0)
        s = self.first + lax.broadcasted_iota(jnp.int32, shape, 0 if flipped else 1)
        ok = t >= s
        for a in self.starts(r):
            ok = ok & ((t < a) | (s >= a))
        return jnp.where(ok, 1.0, 0.0)

    def from_before(self, r, width):
        t = self.first + lax.broadcasted_iota(jnp.int32, (self.length, width), 0)
        ok = t >= 0
        for a in self.starts(r):
            ok = ok & ((a < self.first) | (t < a))
        return jnp.where(ok, 1.0, 0.0)

    def to_after(self, r, width):
        s = self.first + lax.broadcasted_iota(jnp.int32, (self.length, width), 0)
        last = self.first + self.length - 1
        ok = s >= 0
        for a in self.starts(r):
            ok = ok & ((s >= a) | (a > last))
        return jnp.where(ok, 1.0, 0.0)


def assemble(me, pieces, high, low):
    for j, piece in enumerate(pieces):
        rows = piece.shape[-2]
        at = pl.ds(pl.multiple_of((me ^ j) * rows, rows), rows)
        for lead in range(piece.shape[0]):
            h, l = split(piece[lead])
            high[lead, at, :] = h
            low[lead, at, :] = l


def state_blocks(ref, r, p):
    at = (r * PAIRS + p) * HEAD_DIM
    packed = ref[at : at + HEAD_DIM, :]
    sums = ref.shape[0] // (HEAD_DIM + 1) * HEAD_DIM + r * PAIRS + p
    return (
        jnp.concatenate([pick(packed, 0), pick(packed, 1)], axis=0),
        ref[sums : sums + 1, :],
    )


def store_state(ref, r, p, full, key_sum):
    at = (r * PAIRS + p) * HEAD_DIM
    top, bottom = full[:HEAD_DIM], full[HEAD_DIM:]
    ref[at : at + HEAD_DIM, :] = jnp.where(first_head(top.shape), top, bottom)
    sums = ref.shape[0] // (HEAD_DIM + 1) * HEAD_DIM + r * PAIRS + p
    ref[sums : sums + 1, :] = key_sum


def pair_slices(length, r, p):
    return slice(r * length, (r + 1) * length), slice(p * LANES, (p + 1) * LANES)


def keys_kernel(n, slots, rows, info, x, vec, *refs):
    pieces, (nh, nl, k, v, state, wh, wl) = refs[:n], refs[n:]
    length = x.shape[0] // rows
    info = Info(info, length, slots)
    assemble(info.me, pieces, wh, wl)
    unit, _ = normalise(x[...])
    normed = split(unit * vec[0:1, :] + vec[1:2, :])
    nh[...], nl[...] = normed
    k[...] = phi(dot3(normed, (wh[0], wl[0])))
    v[...] = dot3(normed, (wh[1], wl[1]))
    for r in range(rows):
        kept = info.to_after(r, LANES)
        for p in range(PAIRS):
            at = pair_slices(length, r, p)
            masked = k[at] * kept
            full = dot3(split(masked), split(v[at]), 0, 0)
            store_state(state, r, p, full, jnp.sum(masked, axis=0, keepdims=True))


def queries_kernel(n, slots, rows, info, nh, nl, k, v, *refs):
    pieces, (q, numer, denom, wh, wl) = refs[:n], refs[n:]
    length = k.shape[0] // rows
    info = Info(info, length, slots)
    assemble(info.me, pieces, wh, wl)
    q[...] = phi(dot3((nh[...], nl[...]), (wh[0], wl[0])))
    for r in range(rows):
        mask = info.causal(r)
        for p in range(PAIRS):
            at = pair_slices(length, r, p)
            q_pair, v_pair = q[at], v[at]
            keys = split(k[at])
            both = 0.0
            for head in range(2):
                scores = dot3(split(pick(q_pair, head)), keys, 1, 1) * mask
                ones = pick(jnp.ones_like(v_pair), head)
                wide = jnp.concatenate([pick(v_pair, head), ones], axis=1)
                both = both + dot3(split(scores), split(wide))
            numer[at] = both[:, :LANES]
            denom[at] = both[:, LANES:]


def attend_kernel(n, slots, rows, info, x, vec, q, numer, denom, state, *refs):
    pieces, (att, inv, resid, sh, sl, wh, wl) = refs[:n], refs[n:]
    length = x.shape[0] // rows
    info = Info(info, length, slots)
    assemble(info.me, pieces, wh, wl)
    ones = block_ones()
    for r in range(rows):
        use = info.from_before(r, LANES)
        for p in range(PAIRS):
            at = pair_slices(length, r, p)
            block, key_sum = state_blocks(state, r, p)
            q_pair = q[at] * use
            top = numer[at] + dot3(split(q_pair), split(block))
            under = denom[at] + dot2(split(q_pair * key_sum), ones) + EPS_DEN
            inverse = 1.0 / under
            inv[at] = inverse
            att[at] = top * inverse
    result = x[...] + dot3(split(att[...]), (wh[0], wl[0]))
    resid[...] = result
    unit, _ = normalise(result)
    sh[...], sl[...] = split(unit * vec[2:3, :] + vec[3:4, :])


def erf(u):
    return lax.erf(u)


def feed_kernel(vec, bias, sh, sl, dout, resid, uh, ul, dh_, dl_, out, gh, gl, eh, el, dresid, small, dbias, acc, back, oh, ol):
    step, last = pl.program_id(0), pl.num_programs(0) - 1

    @pl.when(step == 0)
    def _():
        oh[...], ol[...] = split(dout[...])

    up, down = (uh[...], ul[...]), (dh_[...], dl_[...])
    h = dot3((sh[...], sl[...]), up) + bias[...]
    cdf = 0.5 * (1.0 + erf(h * math.sqrt(0.5)))
    g = split(h * cdf)
    gh[...], gl[...] = g
    slope = cdf + h * (jnp.exp(-0.5 * h * h) * (1.0 / math.sqrt(2.0 * math.pi)))
    grad = dot3((oh[...], ol[...]), down, 1, 1) * slope
    dbias[...] = jnp.sum(grad, axis=0, keepdims=True)
    e = split(grad)
    eh[...], el[...] = e
    part = dot3(g, down)
    part_back = dot3(e, up, 1, 1)

    @pl.when(step == 0)
    def _():
        acc[...] = part
        back[...] = part_back

    @pl.when(step > 0)
    def _():
        acc[...] += part
        back[...] += part_back

    @pl.when(step == last)
    def _():
        out[...] = resid[...] + acc[...] + vec[4:5, :]
        unit, scale = normalise(resid[...])
        grad_second = back[...]
        small[...] = jnp.zeros_like(small)
        small[2:3, :] = jnp.sum(grad_second * unit, axis=0, keepdims=True)
        small[3:4, :] = jnp.sum(grad_second, axis=0, keepdims=True)
        small[4:5, :] = jnp.sum(dout[...], axis=0, keepdims=True)
        dresid[...] = dout[...] + normalise_back(grad_second * vec[2:3, :], unit, scale)


def attend_back_kernel(slots, rows, info, dresid, wh, wl, q, att, inv, dn, dd, state):
    length = q.shape[0] // rows
    info = Info(info, length, slots)
    grad = dot3(split(dresid[...]), (wh[0], wl[0]), 1, 1)
    dn[...] = grad * inv[...]
    ones = block_ones()
    for r in range(rows):
        use = info.from_before(r, LANES)
        for p in range(PAIRS):
            at = pair_slices(length, r, p)
            lanes = at[1]
            inner = dot2(split(grad[at[0], lanes] * att[at]), ones)
            under = -inner * inv[at]
            dd[at] = under
            q_pair = q[at] * use
            full = dot3(split(q_pair), split(dn[at]), 0, 0)
            store_state(state, r, p, full, jnp.sum(q_pair * under, axis=0, keepdims=True))


def down_grad_kernel(gh, gl, dout, theirs, mine, oh, ol):
    step, half = pl.program_id(0), pl.num_programs(0) // 2

    @pl.when(step == 0)
    def _():
        oh[...], ol[...] = split(dout[...])

    grad = dot3((gh[...], gl[...]), (oh[...], ol[...]), 0, 0)

    @pl.when(step < half)
    def _():
        theirs[0] = grad

    @pl.when(step >= half)
    def _():
        mine[0] = grad


def up_grad_kernel(n, info, sh, sl, eh, el, theirs, mine, full):
    me = info[0]
    full[...] = dot3((sh[...], sl[...]), (eh[...], el[...]), 0, 0)
    rows = full.shape[0] // n
    for j in range(n):
        at = pl.ds(pl.multiple_of((me ^ j) * rows, rows), rows)
        (theirs if j & 1 else mine)[j // 2, 0] = full[at, :]


def deal(me, n, full, theirs, mine, slot):
    rows = full.shape[0] // n
    for j in range(n):
        at = pl.ds(pl.multiple_of((me ^ j) * rows, rows), rows)
        (theirs if j & 1 else mine)[j // 2, slot] = full[at, :]


def local_back_kernel(n, slots, rows, info, nh, nl, q, k, v, dn, dd, state, att, dresid, wh, wl, dk, dv, dnormed, theirs, mine, dq, full):
    length = q.shape[0] // rows
    info = Info(info, length, slots)
    for r in range(rows):
        use = info.from_before(r, LANES)
        mask, flipped = info.causal(r), info.causal(r, True)
        for p in range(PAIRS):
            at = pair_slices(length, r, p)
            q_pair, k_pair, v_pair, dn_pair, dd_pair = q[at], k[at], v[at], dn[at], dd[at]
            block, key_sum = state_blocks(state, r, p)
            grad_q = use * (dot3(split(dn_pair), split(block), 1, 1) + dd_pair * key_sum)
            grad_k = grad_v = 0.0
            keys = split(k_pair)
            values = split(jnp.concatenate([v_pair, jnp.full_like(v_pair, 1.0 / HEAD_DIM)], axis=1))
            both = jnp.concatenate([dn_pair, dd_pair], axis=1)
            for head in range(2):
                tops = split(pick(both, head))
                queries = split(pick(q_pair, head))
                tops_n = (tops[0][:, :LANES], tops[1][:, :LANES])
                grad_scores = dot3(tops, values, 1, 1) * mask
                grad_q = grad_q + dot3(split(grad_scores), split(pick(k_pair, head)))
                grad_flipped = dot3(values, tops, 1, 1) * flipped
                grad_k = grad_k + dot3(split(grad_flipped), queries)
                scores_flipped = dot3(keys, queries, 1, 1) * flipped
                grad_v = grad_v + dot3(split(scores_flipped), tops_n)
            dq[at] = grad_q * jnp.minimum(q_pair, 1.0)
            dk[at] = grad_k
            dv[at] = grad_v
    normed = (nh[...], nl[...])
    grads = split(dq[...])
    dnormed[...] = dot3(grads, (wh[0], wl[0]), 1, 1)
    full[...] = dot3(normed, grads, 0, 0)
    deal(info.me, n, full, theirs, mine, 0)
    full[...] = dot3(split(att[...]), split(dresid[...]), 0, 0)
    deal(info.me, n, full, theirs, mine, 1)


def keys_back_kernel(n, slots, rows, info, x, vec, nh, nl, k, v, dk, dv, dnormed, dresid, state, wh, wl, small_in, dbias, dx, theirs, mine, small, gk, gv, full):
    length = k.shape[0] // rows
    info = Info(info, length, slots)
    for r in range(rows):
        kept = info.to_after(r, LANES)
        for p in range(PAIRS):
            at = pair_slices(length, r, p)
            block, key_sum = state_blocks(state, r, p)
            blocks = split(block)
            k_pair = k[at]
            grad_k = dk[at] + kept * (dot3(split(v[at]), blocks, 1, 1) + key_sum)
            gk[at] = grad_k * jnp.minimum(k_pair, 1.0)
            gv[at] = dv[at] + dot3(split(k_pair * kept), blocks)
    normed = (nh[...], nl[...])
    keys, values = split(gk[...]), split(gv[...])
    full[...] = dot3(normed, keys, 0, 0)
    deal(info.me, n, full, theirs, mine, 0)
    full[...] = dot3(normed, values, 0, 0)
    deal(info.me, n, full, theirs, mine, 1)
    grad = dnormed[...] + dot3(keys, (wh[0], wl[0]), 1, 1) + dot3(values, (wh[1], wl[1]), 1, 1)
    unit, scale = normalise(x[...])
    dx[...] = dresid[...] + normalise_back(grad * vec[0:1, :], unit, scale)
    small[...] = small_in[...]
    small[0:1, :] = jnp.sum(grad * unit, axis=0, keepdims=True)
    small[1:2, :] = jnp.sum(grad, axis=0, keepdims=True)
    width = small.shape[1]
    for i in range(dbias.shape[1] // width):
        small[5 + i : 6 + i, :] = dbias[0:1, i * width : (i + 1) * width]


def call(kernel, outs, args, scratch=(), specs=None, **kw):
    specs = specs or [VMEM] * len(args)
    return pl.pallas_call(
        kernel,
        out_shape=outs,
        in_specs=specs,
        out_specs=[VMEM] * len(outs),
        scratch_shapes=list(scratch),
        compiler_params=pltpu.CompilerParams(vmem_limit_bytes=LIMIT),
        **kw,
    )(*args)


def shaped(shape, dtype=F32):
    return jax.ShapeDtypeStruct(tuple(shape), dtype)


def swap(part, axis, bit):
    return lax.ppermute(part, axis, [(i, i ^ bit) for i in range(lax.axis_size(axis))])


def bits_of(axis):
    return [1 << i for i in range(lax.axis_size(axis).bit_length() - 1)]


def gather_rows(part):
    pieces = {0: part}
    for bit in reversed(bits_of("rows")):
        pieces.update({j ^ bit: swap(piece, "rows", bit) for j, piece in pieces.items()})
    return [pieces[j] for j in range(len(pieces))]


def entering(part, end_docs, prev_doc, reverse):
    place = lax.axis_index("seq")
    rows = end_docs.shape[0]
    total, prefix = part, jnp.zeros_like(part)
    sums = part.shape[0] // (HEAD_DIM + 1)
    row_of = jnp.arange(part.shape[0])
    row_of = jnp.where(row_of < sums * HEAD_DIM, row_of // (PAIRS * HEAD_DIM), (row_of - sums * HEAD_DIM) // PAIRS)

    def at(place):
        return lax.dynamic_index_in_dim(end_docs, place, 1, False)

    def scaled(flag, array):
        column = sum(jnp.where(row_of == r, flag[r], 0.0) for r in range(rows))
        return column[:, None] * array

    for bit in bits_of("seq"):
        other = swap(total, "seq", bit)
        mine_late = ((place & bit) != 0) != reverse
        low = place & ~(bit - 1)
        edge = (lambda group: group) if reverse else (lambda group, bit=bit: group + bit - 1)
        my_edge, other_edge = at(edge(low)), at(edge(low ^ bit))
        prefix = prefix + scaled(jnp.where(mine_late & (other_edge == prev_doc), 1.0, 0.0), other)
        same = jnp.where(my_edge == other_edge, 1.0, 0.0)
        total = scaled(jnp.where(mine_late, 1.0, same), total) + scaled(
            jnp.where(mine_late, same, 1.0), other
        )
    return prefix


def sum_scatter(theirs, mine, extra):
    seq_place = lax.axis_index("seq")
    held = mine + swap(theirs, "rows", 1)
    if extra is not None:
        extra = extra + swap(extra, "rows", 1)
    for bit in bits_of("rows")[1:]:
        held = held.reshape((-1, 2) + held.shape[1:])
        held = held[:, 0] + swap(held[:, 1], "rows", bit)
        if extra is not None:
            extra = extra + swap(extra, "rows", bit)
    held = held[0]
    for bit in bits_of("seq"):
        half = held.shape[0] // 2
        late = ((seq_place & bit) != 0).astype(jnp.int32)
        got = swap(lax.dynamic_slice_in_dim(held, (1 - late) * half, half, 0), "seq", bit)
        held = lax.dynamic_slice_in_dim(held, late * half, half, 0) + got
        if extra is not None:
            extra = extra + swap(extra, "seq", bit)
    for bit in reversed(bits_of("seq")):
        got = swap(held, "seq", bit)
        late = (seq_place & bit) != 0
        held = jnp.where(late, jnp.concatenate([got, held]), jnp.concatenate([held, got]))
    return held, extra


def adamw_step(weight, gradient, first_m, second_m, factor, rate, decay):
    clipped = gradient * factor
    new_m = BETA_ONE * first_m + (1.0 - BETA_ONE) * clipped
    new_v = BETA_TWO * second_m + (1.0 - BETA_TWO) * clipped * clipped
    moved = new_m / (1.0 - BETA_ONE**STEP) / (jnp.sqrt(new_v / (1.0 - BETA_TWO**STEP)) + EPS_ADAM)
    return (clipped, weight - rate * (moved + decay * weight), new_m, new_v)


def body(
    activations,
    cotangent,
    seq_starts,
    attn_weight,
    up_weight,
    down_weight,
    vectors,
    attn_m,
    up_m,
    down_m,
    vec_m,
    attn_v,
    up_v,
    down_v,
    vec_v,
):
    rows, length, width = activations.shape
    n = lax.axis_size("rows")
    hidden = up_weight.shape[1]
    tokens = rows * length
    slots = seq_starts.shape[1]
    block = width // n
    me, place = lax.axis_index("rows"), lax.axis_index("seq")
    first = place * length
    info = jnp.concatenate(
        [jnp.stack([me, place, first]).astype(jnp.int32), seq_starts.reshape(-1)]
    )

    edges = jnp.arange(lax.axis_size("seq"), dtype=jnp.int32) * length

    def docs_at(positions):
        return jnp.sum(
            (seq_starts[:, None, :] <= positions[None, :, None]).astype(jnp.int32), axis=2
        )

    end_docs, begin_docs = docs_at(edges + length - 1), docs_at(edges - 1)
    prev_doc = lax.dynamic_index_in_dim(begin_docs, place, 1, False)
    last_doc = lax.dynamic_index_in_dim(end_docs, place, 1, False)

    x = activations.reshape(tokens, width)
    dout = cotangent.reshape(tokens, width)
    state_shape = shaped((rows * PAIRS * (HEAD_DIM + 1), LANES))
    act, half = shaped((tokens, width)), shaped((tokens, width), BF16)

    def matrix(count):
        return [shaped((count, width, width), BF16)] * 2

    kv_pieces = gather_rows(attn_weight[1:3])
    q_pieces = gather_rows(attn_weight[0:1])
    o_pieces = gather_rows(attn_weight[3:4])
    up_pieces = gather_rows(up_weight[None])
    down_pieces = gather_rows(down_weight[None])

    nh, nl, k, v, state, kvh, kvl = call(
        functools.partial(keys_kernel, n, slots, rows),
        [half, half, act, act, state_shape] + matrix(2),
        [info, x, vectors] + kv_pieces,
        specs=[SMEM] + [VMEM] * (2 + n),
    )
    state_in = entering(state, end_docs, prev_doc, False)
    q, numer, denom, qh, ql = call(
        functools.partial(queries_kernel, n, slots, rows),
        [act, act, act] + matrix(1),
        [info, nh, nl, k, v] + q_pieces,
        specs=[SMEM] + [VMEM] * (4 + n),
    )
    att, inv, resid, sh, sl, oh, ol = call(
        functools.partial(attend_kernel, n, slots, rows),
        [act, act, act, half, half] + matrix(1),
        [info, x, vectors, q, numer, denom, state_in] + o_pieces,
        specs=[SMEM] + [VMEM] * (6 + n),
    )

    def assemble_kernel(info, *refs):
        assemble(info[0], refs[:n], refs[n], refs[n + 1])

    uph, upl = call(
        assemble_kernel,
        [shaped((1, width, hidden), BF16)] * 2,
        [info] + up_pieces,
        specs=[SMEM] + [VMEM] * n,
    )
    dnh, dnl = call(
        assemble_kernel,
        [shaped((1, hidden, width), BF16)] * 2,
        [info] + down_pieces,
        specs=[SMEM] + [VMEM] * n,
    )
    wide = min(512, hidden)
    steps = hidden // wide
    whole = lambda shape: pl.BlockSpec(shape, lambda j: (0,) * len(shape))
    across = pl.BlockSpec((tokens, wide), lambda j: (0, j))
    up_block = pl.BlockSpec((width, wide), lambda j: (0, j))
    down_block = pl.BlockSpec((wide, width), lambda j: (j, 0))
    flat = whole((tokens, width))
    row = pl.BlockSpec((1, wide), lambda j: (0, j))
    out, gh, gl, eh, el, dresid, small, dbias = pl.pallas_call(
        feed_kernel,
        grid=(steps,),
        in_specs=[whole(vectors.shape), row, flat, flat, flat, flat]
        + [up_block] * 2
        + [down_block] * 2,
        out_specs=[flat, across, across, across, across, flat, whole((16, width)), row],
        out_shape=[act]
        + [shaped((tokens, hidden), BF16)] * 4
        + [act, shaped((16, width)), shaped((1, hidden))],
        scratch_shapes=[pltpu.VMEM((tokens, width), F32)] * 2
        + [pltpu.VMEM((tokens, width), BF16)] * 2,
        compiler_params=pltpu.CompilerParams(vmem_limit_bytes=LIMIT),
    )(vectors, vectors[5:].reshape(1, hidden), sh, sl, dout, resid, uph[0], upl[0], dnh[0], dnl[0])

    dn, dd, dstate = call(
        functools.partial(attend_back_kernel, slots, rows),
        [act, act, state_shape],
        [info, dresid, oh, ol, q, att, inv],
        specs=[SMEM] + [VMEM] * 6,
    )
    dstate_in = entering(dstate, begin_docs, last_doc, True)

    share = hidden // n

    def block_of(j, half):
        return jnp.where(j < half, 2 * j + 1, 2 * (j - half))

    down_theirs, down_mine = pl.pallas_call(
        lambda info, *refs: down_grad_kernel(*refs),
        grid_spec=pltpu.PrefetchScalarGridSpec(
            num_scalar_prefetch=1,
            grid=(n,),
            in_specs=[
                pl.BlockSpec((tokens, share), lambda j, info: (0, info[0] ^ block_of(j, n // 2)))
            ]
            * 2
            + [pl.BlockSpec((tokens, width), lambda j, info: (0, 0))],
            out_specs=[
                pl.BlockSpec((1, share, width), lambda j, info: (jnp.minimum(j, n // 2 - 1), 0, 0)),
                pl.BlockSpec((1, share, width), lambda j, info: (jnp.maximum(j - n // 2, 0), 0, 0)),
            ],
            scratch_shapes=[pltpu.VMEM((tokens, width), BF16)] * 2,
        ),
        out_shape=[shaped((n // 2, share, width))] * 2,
        compiler_params=pltpu.CompilerParams(vmem_limit_bytes=LIMIT),
    )(info, gh, gl, dout)
    up_out = pl.BlockSpec((n // 2, 1, block, wide), lambda j: (0, j, 0, 0))
    up_theirs, up_mine = pl.pallas_call(
        functools.partial(up_grad_kernel, n),
        grid=(steps,),
        in_specs=[SMEM, flat, flat, across, across],
        out_specs=[up_out, up_out],
        out_shape=[shaped((n // 2, steps, block, wide))] * 2,
        scratch_shapes=[pltpu.VMEM((width, wide), F32)],
        compiler_params=pltpu.CompilerParams(vmem_limit_bytes=LIMIT),
    )(info, sh, sl, eh, el)

    pair = shaped((n // 2, 2, block, width))
    dk, dv, dnormed, qo_theirs, qo_mine = call(
        functools.partial(local_back_kernel, n, slots, rows),
        [act, act, act, pair, pair],
        [info, nh, nl, q, k, v, dn, dd, state_in, att, dresid, qh, ql],
        scratch=[pltpu.VMEM((tokens, width), F32), pltpu.VMEM((width, width), F32)],
        specs=[SMEM] + [VMEM] * 12,
    )
    dx, kv_theirs, kv_mine, small = call(
        functools.partial(keys_back_kernel, n, slots, rows),
        [act, pair, pair, shaped((16, width))],
        [info, x, vectors, nh, nl, k, v, dk, dv, dnormed, dresid, dstate_in, kvh, kvl, small, dbias],
        scratch=[pltpu.VMEM((tokens, width), F32)] * 2 + [pltpu.VMEM((width, width), F32)],
        specs=[SMEM] + [VMEM] * 15,
    )

    def rowed(a):
        return a.reshape(n // 2, -1, width)

    sum_down, _ = sum_scatter(rowed(down_theirs), rowed(down_mine), None)
    sum_up, _ = sum_scatter(rowed(up_theirs), rowed(up_mine), None)
    sum_qo, _ = sum_scatter(rowed(qo_theirs), rowed(qo_mine), None)
    sum_kv, total_small = sum_scatter(rowed(kv_theirs), rowed(kv_mine), small)
    total_vec = total_small[: vectors.shape[0]]
    sum_qo, sum_kv = (a.reshape(2, block, width) for a in (sum_qo, sum_kv))
    shard_attn = jnp.stack([sum_qo[0], sum_kv[0], sum_kv[1], sum_qo[1]])
    shard_up = jnp.swapaxes(sum_up.reshape(steps, block, wide), 0, 1).reshape(block, hidden)
    shard_down = sum_down

    part_square = (
        jnp.sum(shard_attn * shard_attn)
        + jnp.sum(shard_up * shard_up)
        + jnp.sum(shard_down * shard_down)
    )
    for bit in bits_of("rows"):
        part_square = part_square + swap(part_square, "rows", bit)
    square = part_square + jnp.sum(total_vec * total_vec)
    grad_norm = jnp.sqrt(square)
    factor = jnp.minimum(1.0, CLIP_AT / (grad_norm + 1e-06))
    attn_g, attn_new, attn_m_new, attn_v_new = adamw_step(
        attn_weight, shard_attn, attn_m, attn_v, factor, RATE_MAT, DECAY_MAT
    )
    up_g, up_new, up_m_new, up_v_new = adamw_step(
        up_weight, shard_up, up_m, up_v, factor, RATE_MAT, DECAY_MAT
    )
    down_g, down_new, down_m_new, down_v_new = adamw_step(
        down_weight, shard_down, down_m, down_v, factor, RATE_MAT, DECAY_MAT
    )
    vec_g, vec_new, vec_m_new, vec_v_new = adamw_step(
        vectors, total_vec, vec_m, vec_v, factor, RATE_VEC, 0.0
    )
    return (
        out.reshape(activations.shape),
        dx.reshape(activations.shape),
        grad_norm,
        attn_g,
        up_g,
        down_g,
        vec_g,
        attn_new,
        up_new,
        down_new,
        vec_new,
        attn_m_new,
        up_m_new,
        down_m_new,
        vec_m_new,
        attn_v_new,
        up_v_new,
        down_v_new,
        vec_v_new,
    )


def solution(mesh):
    stretch = P("rows", "seq", None)
    stacked = P(None, "rows", None)
    split_rows = P("rows", None)
    weights = (stacked, split_rows, split_rows, P())
    return jax.shard_map(
        body,
        mesh=mesh,
        in_specs=(stretch, stretch, split_rows) + weights * 3,
        out_specs=(stretch, stretch, P()) + weights * 4,
        check_vma=False,
    )
```

time: 628 us -> 418 us (0.67)
  matrix products: 154 us -> 0 us
  blocking collectives: 122 us -> 0 us
  Pallas kernels: 0 us -> 114 us
  waiting for transfers between devices: 253 us -> 166 us
  starting transfers between devices: 0.45 us -> 67.7 us
  between operations: 19.1 us -> 6.56 us
  other arithmetic: 49 us -> 39 us
    ppermute x0 -> x60, waiting for transfers between devices: none -> 166 us  [swap(): lax.ppermute(part, axis, [(i, i ^ bit) for i in range(lax.axis_size(axis))])]
    psum x1 -> x0, waiting for transfers between devices: 163 us -> none  [body(): lax.psum((grad_attn, grad_up, grad_down, grad_vec), ('seq', 'rows'))]
    dot_general x32 -> x0, matrix products: 154 us -> none  [the longest x3 41.9 us: finish(): jnp.dot(jax.nn.gelu(upped, approximate=False), down_matrix, precision=PRE...]
    pallas_call x0 -> x11, Pallas kernels: none -> 114 us  [the longest x8 76.5 us: call(): pl.pallas_call(kernel, out_shape=outs, in_specs=specs, out_specs=[VMEM] *...]
    all_gather x5 -> x0, waiting for transfers between devices: 87.6 us -> none  [the longest x1 31.6 us: body(): lax.all_gather(attn_weight, 'rows', axis=1, tiled=True)]
    all_gather x3 -> x0, blocking collectives: 83.5 us -> none  [entering(): gathered = jax.tree.map(lambda a: lax.all_gather(a, axis), part)]
    ppermute x0 -> x60, starting transfers between devices: none -> 67.7 us  [swap(): lax.ppermute(part, axis, [(i, i ^ bit) for i in range(lax.axis_size(axis))])]
    psum x1 -> x0, blocking collectives: 38.9 us -> none  [body(): lax.psum((grad_attn, grad_up, grad_down, grad_vec), ('seq', 'rows'))]
  transfers between devices with their start and end apart: 6 -> 60, of which waited for: 6 -> 28; matrix products, arithmetic and copies ran while one was open for 18% -> 10% of each run, Pallas kernels for 0% -> 20%
where the time goes in v1:
time: 418 us; the launch traced here: 414 us
  waiting for transfers between devices  166 us (40%)
  Pallas kernels  114 us (27%)
  starting transfers between devices  67.7 us (16%)
  other arithmetic  39 us (9%)
  local copies, waits for them, and re-layouts  21.3 us (5%)
  between operations  6.56 us (2%)
    ppermute x60, waiting for transfers between devices, swap(): lax.ppermute(part, axis, [(i, i ^ bit) for i in range(lax.axis_size(axis))])  166 us
    pallas_call x8, Pallas kernels, call(): pl.pallas_call(kernel, out_shape=outs, in_specs=specs, out_specs=[VMEM] *...  76.5 us
    ppermute x60, starting transfers between devices, swap(): lax.ppermute(part, axis, [(i, i ^ bit) for i in range(lax.axis_size(axis))])  67.7 us
    pallas_call x1, Pallas kernels, body(): pl.pallas_call(feed_kernel, grid=(steps,), in_specs=[whole(vectors.shape)...  20.8 us
    add x8, other arithmetic, scaled(): column = sum((jnp.where(row_of == r, flag[r], 0.0) for r in range(rows)))  18 us
    unnamed x73, local copies, waits for them, and re-layouts  10.5 us
    pallas_call x1, Pallas kernels, body(): pl.pallas_call(lambda info, *refs: down_grad_kernel(*refs), grid_spec=plt...  8.56 us
  transfers between devices with their start and end apart: 60, of which 28 were waited for; matrix products, arithmetic and copies ran while one was open for 10% of the time, Pallas kernels for 20%

profile of v1, /device:TPU:0, one launch (start us, length us, event | category | flops | bytes accessed | tf_op | source)
XLA Modules:
  0.0 414.3 jit_solution(4148495737503929012)
XLA Ops:
  8.7 9.2 %collective-permute-done.1.refs_2_ = f32[2,128,512]{2,1,0:T(8,128)} collective-permute-done((f32[2,128,512]{2,1,0:T(8,128)S(1)}, f32[2,128,512]{2,1,0:T(8,128)}, u32[]{:S(2)}, u32[]{:S(2)}) %collective-permute-start.1) | collective-permute-done | bytes 524320 | tf_op jit(solution)/shard_map/ppermute | solution.py:395
  23.9 5.6 %shard_map.294 = (bf16[512,512]{1,0:T(8,128)(2,1)}, bf16[512,512]{1,0:T(8,128)(2,1)}, f32[512,512]{1,0:T(8,128)}, f32[512,512]{1,0:T(8,128)}, f32[520,128]{1,0:T...) custom-call(s32[9]{0:T(128)} %pad_add_fusion.info, f32[512,512]{1,0:T(8,128)} %bitcast.112, ...), custom_call_target="tpu_custom_call" | custom-call | tf_op jit(solution)/shard_map/pallas_call | solution.py:379
  46.7 26.4 %collective-permute-done.10.refs_2_ = f32[1,128,512]{2,1,0:T(8,128)} collective-permute-done((f32[1,128,512]{2,1,0:T(8,128)S(1)}, f32[1,128,512]{2,1,0:T(8,128)}, u32[]{:S(2)}, u32[]{:S(2)}) %collective-permute-start.10) | collective-permute-done | bytes 262176 | tf_op jit(solution)/shard_map/ppermute | solution.py:395
  75.1 4.5 %collective-permute-done.5.refs_3_ = f32[1,128,512]{2,1,0:T(8,128)S(1)} collective-permute-done((f32[1,128,512]{2,1,0:T(8,128)S(1)}, f32[1,128,512]{2,1,0:T(8,128)S(1)}, u32[]{:S(2)}, u32[]{:S(2)}) %collective-permute-start.5) | collective-permute-done | bytes 262176 | tf_op jit(solution)/shard_map/ppermute | solution.py:395
  83.7 11.0 %collective-permute-done.8 = f32[520,128]{1,0:T(8,128)S(1)} collective-permute-done((f32[520,128]{1,0:T(8,128)S(1)}, f32[520,128]{1,0:T(8,128)S(1)}, u32[]{:S(2)}, u32[]{:S(2)}) %collective-permute-start.8) | collective-permute-done | bytes 266272 | tf_op jit(solution)/shard_map/ppermute | solution.py:395
  96.7 8.2 %shard_map.295 = (f32[512,512]{1,0:T(8,128)}, f32[512,512]{1,0:T(8,128)}, f32[512,512]{1,0:T(8,128)}, bf16[1,512,512]{2,1,0:T(8,128)(2,1)}, bf16[1,512,512]{2,1,0:T(8,128)(2,1)}) custom-call(s32[9]{0:T(128)} %pad_add_fusion.info, bf16[512,512]{1,0:T(8,128)(2,1)} %get-tuple-element.66.nh, bf16[512,512]{1,0:T(8,128)(2,1)} %get-tuple-element.67.nl, ...), custom_call_target="tpu_custom_call" | custom-call | tf_op jit(solution)/shard_map/pallas_call | solution.py:379
  106.7 6.0 %shard_map.296 = (f32[512,512]{1,0:T(8,128)}, f32[512,512]{1,0:T(8,128)}, f32[512,512]{1,0:T(8,128)}, bf16[512,512]{1,0:T(8,128)(2,1)}, bf16[512,512]{1,0:T(8,12...) custom-call(s32[9]{0:T(128)} %pad_add_fusion.info, f32[512,512]{1,0:T(8,128)} %bitcast.113, ...), custom_call_target="tpu_custom_call" | custom-call | tf_op jit(solution)/shard_map/pallas_call | solution.py:379
  114.6 16.1 %shard_map.297 = (bf16[1,512,2048]{2,1,0:T(8,128)(2,1)}, bf16[1,512,2048]{2,1,0:T(8,128)(2,1)}) custom-call(s32[9]{0:T(128)} %pad_add_fusion.info, f32[1,128,2048]{2,1,0:T(8,128)} %bitcast.117, f32[1,128,2048]{2,1,0:T(8,128)} %copy-done.19, f32[1,128,2048]{2,1,0:T(8,128)} %collective-permute-done.13.refs_2_, f32[1,128,2048]{2,1,0:T(8,128)} %copy-done.21), custom_call_target="tpu_custom_call" | custom-call | tf_op jit(solution)/shard_map/pallas_call | solution.py:379
  132.6 4.6 %shard_map.298 = (bf16[1,2048,512]{2,1,0:T(8,128)(2,1)}, bf16[1,2048,512]{2,1,0:T(8,128)(2,1)}) custom-call(s32[9]{0:T(128)} %pad_add_fusion.info, f32[1,512,512]{2,1,0:T(8,128)} %bitcast.120, f32[1,512,512]{2,1,0:T(8,128)} %copy-done.18, f32[1,512,512]{2,1,0:T(8,128)} %collective-permute-done.16.refs_2_, f32[1,512,512]{2,1,0:T(8,128)} %copy-done.20), custom_call_target="tpu_custom_call" | custom-call | tf_op jit(solution)/shard_map/pallas_call | solution.py:379
  137.2 20.8 %shard_map.299 = (f32[512,512]{1,0:T(8,128)}, bf16[512,2048]{1,0:T(8,128)(2,1)}, bf16[512,2048]{1,0:T(8,128)(2,1)}, bf16[512,2048]{1,0:T(8,128)(2,1)}, bf16[512,...) custom-call(f32[9,512]{1,0:T(8,128)} %vec.7, f32[1,2048]{1,0:T(1,128)} %bitcast.136, ...), custom_call_target="tpu_custom_call" | custom-call | tf_op jit(solution)/shard_map/pallas_call | solution.py:568
  158.0 5.5 %shard_map.300 = (f32[512,512]{1,0:T(8,128)}, f32[512,512]{1,0:T(8,128)}, f32[520,128]{1,0:T(8,128)}) custom-call(s32[9]{0:T(128)} %pad_add_fusion.info, f32[512,512]{1,0:T(8,128)} %get-tuple-element.82.dresid, bf16[1,512,512]{2,1,0:T(8,128)(2,1)} %get-tuple-element.83.wh, bf16[1,512,512]{2,1,0:T(8,128)(2,1)} %get-tuple-element.84.wl, ...), custom_call_target="tpu_custom_call" | custom-call | tf_op jit(solution)/shard_map/pallas_call | solution.py:379
  165.6 20.6 %shard_map.301 = (f32[512,512]{1,0:T(8,128)}, f32[512,512]{1,0:T(8,128)}, f32[512,512]{1,0:T(8,128)}, f32[2,2,128,512]{3,2,1,0:T(8,128)}, f32[2,2,128,512]{3,2,1,0:T(8,128)}) custom-call(s32[9]{0:T(128)} %pad_add_fusion.info, bf16[512,512]{1,0:T(8,128)(2,1)} %get-tuple-element.66.nh, bf16[512,512]{1,0:T(8,128)(2,1)} %get-tuple-element.67.nl, ...), custom_call_target="tpu_custom_call" | custom-call | tf_op jit(solution)/shard_map/pallas_call | solution.py:379
  194.1 4.3 %collective-permute-done.19 = f32[520,128]{1,0:T(8,128)S(1)} collective-permute-done((f32[520,128]{1,0:T(8,128)S(1)}, f32[520,128]{1,0:T(8,128)S(1)}, u32[]{:S(2)}, u32[]{:S(2)}) %collective-permute-start.19) | collective-permute-done | bytes 266272 | tf_op jit(solution)/shard_map/ppermute | solution.py:395
  207.5 5.6 %collective-permute-done.20 = f32[520,128]{1,0:T(8,128)S(1)} collective-permute-done((f32[520,128]{1,0:T(8,128)S(1)}, f32[520,128]{1,0:T(8,128)S(1)}, u32[]{:S(2)}, u32[]{:S(2)}) %collective-permute-start.20) | collective-permute-done | bytes 266272 | tf_op jit(solution)/shard_map/ppermute | solution.py:395
  214.0 9.9 %shard_map.302 = (f32[512,512]{1,0:T(8,128)}, f32[2,2,128,512]{3,2,1,0:T(8,128)}, f32[2,2,128,512]{3,2,1,0:T(8,128)}, f32[16,512]{1,0:T(8,128)}) custom-call(s32[9]{0:T(128)} %pad_add_fusion.info, f32[512,512]{1,0:T(8,128)} %bitcast.114, f32[9,512]{1,0:T(8,128)} %vec.7, bf16[512,512]{1,0:T(8,128)(2,1)} %get-tuple-element.66.nh, ...), custom_call_target="tpu_custom_call" | custom-call | tf_op jit(solution)/shard_map/pallas_call | solution.py:379
  224.0 8.6 %shard_map.304 = (f32[2,512,512]{2,1,0:T(8,128)}, f32[2,512,512]{2,1,0:T(8,128)}) custom-call(s32[9]{0:T(128)} %pad_add_fusion.info, bf16[512,2048]{1,0:T(8,128)(2,1)} %get-tuple-element.108.refs_0_, bf16[512,2048]{1,0:T(8,128)(2,1)} %get-tuple-element.109.refs_1_, f32[512,512]{1,0:T(8,128)} %bitcast.130), custom_call_target="tpu_custom_call" | custom-call | tf_op jit(solution)/shard_map/pallas_call | solution.py:596
  245.4 7.8 %shard_map.303 = (f32[2,4,128,512]{3,2,1,0:T(8,128)}, f32[2,4,128,512]{3,2,1,0:T(8,128)}) custom-call(s32[9]{0:T(128)} %pad_add_fusion.info, bf16[512,512]{1,0:T(8,128)(2,1)} %get-tuple-element.74.sh, bf16[512,512]{1,0:T(8,128)(2,1)} %get-tuple-element.75.sl, bf16[512,2048]{1,0:T(8,128)(2,1)} %get-tuple-element.104.eh, bf16[512,2048]{1,0:T(8,128)(2,1)} %get-tuple-element.105.el), custom_call_target="tpu_custom_call" | custom-call | tf_op jit(solution)/shard_map/pallas_call | solution.py:616
  271.2 6.6 %collective-permute-done.30 = f32[1,256,512]{2,1,0:T(8,128)S(1)} collective-permute-done((f32[1,256,512]{2,1,0:T(8,128)S(1)}, f32[1,256,512]{2,1,0:T(8,128)S(1)}, u32[]{:S(2)}, u32[]{:S(2)}) %collective-permute-start.30) | collective-permute-done | bytes 524320 | tf_op jit(solution)/shard_map/ppermute | solution.py:395
  292.2 8.1 %collective-permute-done.46 = f32[1,512,512]{2,1,0:T(8,128)S(1)} collective-permute-done((f32[1,512,512]{2,1,0:T(8,128)S(1)}, f32[1,512,512]{2,1,0:T(8,128)S(1)}, u32[]{:S(2)}, u32[]{:S(2)}) %collective-permute-start.46) | collective-permute-done | bytes 1048608 | tf_op jit(solution)/shard_map/ppermute | solution.py:395
  302.1 19.1 %collective-permute-done.38 = f32[1,512,512]{2,1,0:T(8,128)S(1)} collective-permute-done((f32[1,512,512]{2,1,0:T(8,128)S(1)}, f32[1,512,512]{2,1,0:T(8,128)S(1)}, u32[]{:S(2)}, u32[]{:S(2)}) %collective-permute-start.38) | collective-permute-done | bytes 1048608 | tf_op jit(solution)/shard_map/ppermute | solution.py:395
  326.7 7.2 %collective-permute-done.39 = f32[256,512]{1,0:T(8,128)S(1)} collective-permute-done((f32[256,512]{1,0:T(8,128)S(1)}, f32[256,512]{1,0:T(8,128)S(1)}, u32[]{:S(2)}, u32[]{:S(2)}) %collective-permute-start.39) | collective-permute-done | bytes 524320 | tf_op jit(solution)/shard_map/ppermute | solution.py:395
  337.6 5.0 %collective-permute-done.40 = f32[128,512]{1,0:T(8,128)S(1)} collective-permute-done((f32[128,512]{1,0:T(8,128)S(1)}, f32[128,512]{1,0:T(8,128)S(1)}, u32[]{:S(2)}, u32[]{:S(2)}) %collective-permute-start.40) | collective-permute-done | bytes 262176 | tf_op jit(solution)/shard_map/ppermute | solution.py:395
  346.4 6.5 %collective-permute-done.41 = f32[64,512]{1,0:T(8,128)S(1)} collective-permute-done((f32[64,512]{1,0:T(8,128)S(1)}, f32[64,512]{1,0:T(8,128)S(1)}, u32[]{:S(2)}, u32[]{:S(2)}) %collective-permute-start.41) | collective-permute-done | bytes 131104 | tf_op jit(solution)/shard_map/ppermute | solution.py:395
  374.7 16.5 %collective-permute-done.44 = f32[256,512]{1,0:T(8,128)S(1)} collective-permute-done((f32[256,512]{1,0:T(8,128)S(1)}, f32[256,512]{1,0:T(8,128)S(1)}, u32[]{:S(2)}, u32[]{:S(2)}) %collective-permute-start.44) | collective-permute-done | bytes 524320 | tf_op jit(solution)/shard_map/ppermute | solution.py:395
  (277 shorter events, 164.1 us)
Async XLA Ops:
  6.1 35.2 %collective-permute-start.4 = (f32[1,128,512]{2,1,0:T(8,128)S(1)}, f32[1,128,512]{2,1,0:T(8,128)S(1)}, u32[]{:S(2)}, u32[]{:S(2)}) collective-permute-start(f32[1,128,512]{2,1,0:T(8,128)S(1)} %get-tuple-element.131.refs_0_), channel_id=1, source_target_pairs={{0,2},{1,3},{2,0},{3,1},{4,6},{5,7},{6,4},{7,5},{8,10},{9,11},{10,... | collective-permute-start | bytes 786440 | tf_op jit(solution)/shard_map/ppermute | solution.py:395
  6.2 67.4 %collective-permute-start.13 = (f32[1,128,2048]{2,1,0:T(8,128)S(1)}, f32[1,128,2048]{2,1,0:T(8,128)}, u32[]{:S(2)}, u32[]{:S(2)}) collective-permute-start(f32[1,128,2048]{2,1,0:T(8,128)S(1)} %bitcast.118), channel_id=1, source_target_pairs={{0,2},{1,3},{2,0},{3,1},{4,6},{5,7},{6,4},{7,5},{8,10},{9,11},{10,... | collective-permute-start | bytes 3145736 | tf_op jit(solution)/shard_map/ppermute | solution.py:395
  8.2 65.6 %collective-permute-start.16 = (f32[1,512,512]{2,1,0:T(8,128)S(1)}, f32[1,512,512]{2,1,0:T(8,128)}, u32[]{:S(2)}, u32[]{:S(2)}) collective-permute-start(f32[1,512,512]{2,1,0:T(8,128)S(1)} %bitcast.121), channel_id=1, source_target_pairs={{0,2},{1,3},{2,0},{3,1},{4,6},{5,7},{6,4},{7,5},{8,10},{9,11},{10,... | collective-permute-start | bytes 3145736 | tf_op jit(solution)/shard_map/ppermute | solution.py:395
  38.4 34.8 %collective-permute-start.10 = (f32[1,128,512]{2,1,0:T(8,128)S(1)}, f32[1,128,512]{2,1,0:T(8,128)}, u32[]{:S(2)}, u32[]{:S(2)}) collective-permute-start(f32[1,128,512]{2,1,0:T(8,128)S(1)} %get-tuple-element.130.refs_0_), channel_id=1, source_target_pairs={{0,2},{1,3},{2,0},{3,1},{4,6},{5,7},{6,4},{7,5},{8,10},{9,11},{10,... | collective-permute-start | bytes 786440 | tf_op jit(solution)/shard_map/ppermute | solution.py:395
  41.3 31.9 %collective-permute-start.9 = (f32[1,128,512]{2,1,0:T(8,128)S(1)}, f32[1,128,512]{2,1,0:T(8,128)}, u32[]{:S(2)}, u32[]{:S(2)}) collective-permute-start(f32[1,128,512]{2,1,0:T(8,128)S(1)} %get-tuple-element.130.refs_0_), channel_id=1, source_target_pairs={{0,1},{1,0},{2,3},{3,2},{4,5},{5,4},{6,7},{7,6},{8,9},{9,8},{10,11... | collective-permute-start | bytes 786440 | tf_op jit(solution)/shard_map/ppermute | solution.py:395
  41.4 32.8 %collective-permute-start.7 = (f32[520,128]{1,0:T(8,128)S(1)}, f32[520,128]{1,0:T(8,128)S(1)}, u32[]{:S(2)}, u32[]{:S(2)}) collective-permute-start(f32[520,128]{1,0:T(8,128)S(1)} %multiply_add_fusion.8), channel_id=1, source_target_pairs={{0,8},{4,12},{8,0},{12,4},{16,24},{20,28},{24,16},{28,20},{1,9},{5... | collective-permute-start | bytes 798728 | tf_op jit(solution)/shard_map/ppermute | solution.py:395
  73.2 39.5 %collective-permute-start.12 = (f32[1,128,2048]{2,1,0:T(8,128)S(1)}, f32[1,128,2048]{2,1,0:T(8,128)S(1)}, u32[]{:S(2)}, u32[]{:S(2)}) collective-permute-start(f32[1,128,2048]{2,1,0:T(8,128)S(1)} %bitcast.119), channel_id=1, source_target_pairs={{0,1},{1,0},{2,3},{3,2},{4,5},{5,4},{6,7},{7,6},{8,9},{9,8},{10,11... | collective-permute-start | bytes 3145736 | tf_op jit(solution)/shard_map/ppermute | solution.py:395
  73.2 57.5 %collective-permute-start.15 = (f32[1,512,512]{2,1,0:T(8,128)S(1)}, f32[1,512,512]{2,1,0:T(8,128)S(1)}, u32[]{:S(2)}, u32[]{:S(2)}) collective-permute-start(f32[1,512,512]{2,1,0:T(8,128)S(1)} %bitcast.122), channel_id=1, source_target_pairs={{0,1},{1,0},{2,3},{3,2},{4,5},{5,4},{6,7},{7,6},{8,9},{9,8},{10,11... | collective-permute-start | bytes 3145736 | tf_op jit(solution)/shard_map/ppermute | solution.py:395
  73.8 38.9 %collective-permute-start.14 = (f32[1,128,2048]{2,1,0:T(8,128)}, f32[1,128,2048]{2,1,0:T(8,128)S(1)}, u32[]{:S(2)}, u32[]{:S(2)}) collective-permute-start(f32[1,128,2048]{2,1,0:T(8,128)} %collective-permute-done.13.refs_2_), channel_id=1, source_target_pairs={{0,1},{1,0},{2,3},{3,2},{4,5},{5,4},{6,7},{7,6},{8,9},{9,8},{10,11... | collective-permute-start | bytes 3145736 | tf_op jit(solution)/shard_map/ppermute | solution.py:395
  74.2 56.5 %collective-permute-start.17 = (f32[1,512,512]{2,1,0:T(8,128)}, f32[1,512,512]{2,1,0:T(8,128)S(1)}, u32[]{:S(2)}, u32[]{:S(2)}) collective-permute-start(f32[1,512,512]{2,1,0:T(8,128)} %collective-permute-done.16.refs_2_), channel_id=1, source_target_pairs={{0,1},{1,0},{2,3},{3,2},{4,5},{5,4},{6,7},{7,6},{8,9},{9,8},{10,11... | collective-permute-start | bytes 3145736 | tf_op jit(solution)/shard_map/ppermute | solution.py:395
  163.5 26.0 %collective-permute-start.18 = (f32[520,128]{1,0:T(8,128)}, f32[520,128]{1,0:T(8,128)S(1)}, u32[]{:S(2)}, u32[]{:S(2)}) collective-permute-start(f32[520,128]{1,0:T(8,128)} %get-tuple-element.94), channel_id=1, source_target_pairs={{0,4},{4,0},{8,12},{12,8},{16,20},{20,16},{24,28},{28,24},{1,5},{5... | collective-permute-start | bytes 798728 | tf_op jit(solution)/shard_map/ppermute | solution.py:395
  202.0 31.0 %collective-permute-start.22 = (f32[1,256,512]{2,1,0:T(8,128)}, f32[1,256,512]{2,1,0:T(8,128)}, u32[]{:S(2)}, u32[]{:S(2)}) collective-permute-start(f32[1,256,512]{2,1,0:T(8,128)} %slice_bitcast_fusion.6), channel_id=1, source_target_pairs={{0,2},{1,3},{2,0},{3,1},{4,6},{5,7},{6,4},{7,5},{8,10},{9,11},{10,... | collective-permute-start | bytes 1572872 | tf_op jit(solution)/shard_map/ppermute | solution.py:395
  223.9 33.0 %collective-permute-start.29 = (f32[2,256,512]{2,1,0:T(8,128)}, f32[2,256,512]{2,1,0:T(8,128)}, u32[]{:S(2)}, u32[]{:S(2)}) collective-permute-start(f32[2,256,512]{2,1,0:T(8,128)} %bitcast.140), channel_id=1, source_target_pairs={{0,1},{1,0},{2,3},{3,2},{4,5},{5,4},{6,7},{7,6},{8,9},{9,8},{10,11... | collective-permute-start | bytes 3145736 | tf_op jit(solution)/shard_map/ppermute | solution.py:395
  232.6 36.0 %collective-permute-start.45 = (f32[2,512,512]{2,1,0:T(8,128)}, f32[2,512,512]{2,1,0:T(8,128)S(1)}, u32[]{:S(2)}, u32[]{:S(2)}) collective-permute-start(f32[2,512,512]{2,1,0:T(8,128)} %get-tuple-element.111), channel_id=1, source_target_pairs={{0,1},{1,0},{2,3},{3,2},{4,5},{5,4},{6,7},{7,6},{8,9},{9,8},{10,11... | collective-permute-start | bytes 6291464 | tf_op jit(solution)/shard_map/ppermute | solution.py:395
  235.0 21.7 %collective-permute-start.23 = (f32[128,512]{1,0:T(8,128)S(1)}, f32[128,512]{1,0:T(8,128)S(1)}, u32[]{:S(2)}, u32[]{:S(2)}) collective-permute-start(f32[128,512]{1,0:T(8,128)S(1)} %dynamic-slice_bitcast_fusion.3), channel_id=1, source_target_pairs={{0,4},{4,0},{8,12},{12,8},{16,20},{20,16},{24,28},{28,24},{1,5},{5... | collective-permute-start | bytes 786440 | tf_op jit(solution)/shard_map/ppermute | solution.py:395
  253.3 32.5 %collective-permute-start.59 = (f32[16,512]{1,0:T(8,128)S(1)}, f32[16,512]{1,0:T(8,128)S(1)}, u32[]{:S(2)}, u32[]{:S(2)}) collective-permute-start(f32[16,512]{1,0:T(8,128)S(1)} %add.575), channel_id=1, source_target_pairs={{0,16},{4,20},{8,24},{12,28},{16,0},{20,4},{24,8},{28,12},{1,17},{... | collective-permute-start | bytes 98312 | tf_op jit(solution)/shard_map/ppermute | solution.py:395
  269.1 31.2 %collective-permute-start.46 = (f32[1,512,512]{2,1,0:T(8,128)S(1)}, f32[1,512,512]{2,1,0:T(8,128)S(1)}, u32[]{:S(2)}, u32[]{:S(2)}) collective-permute-start(f32[1,512,512]{2,1,0:T(8,128)S(1)} %slice_bitcast_fusion), channel_id=1, source_target_pairs={{0,2},{1,3},{2,0},{3,1},{4,6},{5,7},{6,4},{7,5},{8,10},{9,11},{10,... | collective-permute-start | bytes 3145736 | tf_op jit(solution)/shard_map/ppermute | solution.py:395
  279.5 41.7 %collective-permute-start.38 = (f32[1,512,512]{2,1,0:T(8,128)S(1)}, f32[1,512,512]{2,1,0:T(8,128)S(1)}, u32[]{:S(2)}, u32[]{:S(2)}) collective-permute-start(f32[1,512,512]{2,1,0:T(8,128)S(1)} %slice_bitcast_fusion.2), channel_id=1, source_target_pairs={{0,2},{1,3},{2,0},{3,1},{4,6},{5,7},{6,4},{7,5},{8,10},{9,11},{10,... | collective-permute-start | bytes 3145736 | tf_op jit(solution)/shard_map/ppermute | solution.py:395
  286.5 74.4 %collective-permute-start.28 = (f32[128,512]{1,0:T(8,128)S(1)}, f32[128,512]{1,0:T(8,128)S(1)}, u32[]{:S(2)}, u32[]{:S(2)}) collective-permute-start(f32[128,512]{1,0:T(8,128)S(1)} %maximum_select_fusion.6), channel_id=1, source_target_pairs={{0,4},{4,0},{8,12},{12,8},{16,20},{20,16},{24,28},{28,24},{1,5},{5... | collective-permute-start | bytes 786440 | tf_op jit(solution)/shard_map/ppermute | solution.py:395
  290.3 32.7 %collective-permute-start.33 = (f32[32,512]{1,0:T(8,128)S(1)}, f32[32,512]{1,0:T(8,128)S(1)}, u32[]{:S(2)}, u32[]{:S(2)}) collective-permute-start(f32[32,512]{1,0:T(8,128)S(1)} %constant_dynamic-slice_fusion.4), channel_id=1, source_target_pairs={{0,16},{4,20},{8,24},{12,28},{16,0},{20,4},{24,8},{28,12},{1,17},{... | collective-permute-start | bytes 196616 | tf_op jit(solution)/shard_map/ppermute | solution.py:395
  300.6 24.7 %collective-permute-start.47 = (f32[256,512]{1,0:T(8,128)S(1)}, f32[256,512]{1,0:T(8,128)S(1)}, u32[]{:S(2)}, u32[]{:S(2)}) collective-permute-start(f32[256,512]{1,0:T(8,128)S(1)} %dynamic-slice_bitcast_fusion), channel_id=1, source_target_pairs={{0,4},{4,0},{8,12},{12,8},{16,20},{20,16},{24,28},{28,24},{1,5},{5... | collective-permute-start | bytes 1572872 | tf_op jit(solution)/shard_map/ppermute | solution.py:395
  322.9 30.0 %collective-permute-start.34 = (f32[32,512]{1,0:T(8,128)S(1)}, f32[32,512]{1,0:T(8,128)S(1)}, u32[]{:S(2)}, u32[]{:S(2)}) collective-permute-start(f32[32,512]{1,0:T(8,128)S(1)} %dynamic-slice_add_fusion.6), channel_id=1, source_target_pairs={{0,16},{4,20},{8,24},{12,28},{16,0},{20,4},{24,8},{28,12},{1,17},{... | collective-permute-start | bytes 196616 | tf_op jit(solution)/shard_map/ppermute | solution.py:395
  367.9 25.5 %collective-permute-start.52 = (f32[256,512]{1,0:T(8,128)S(1)}, f32[256,512]{1,0:T(8,128)S(1)}, u32[]{:S(2)}, u32[]{:S(2)}) collective-permute-start(f32[256,512]{1,0:T(8,128)S(1)} %maximum_select_fusion.5), channel_id=1, source_target_pairs={{0,4},{4,0},{8,12},{12,8},{16,20},{20,16},{24,28},{28,24},{1,5},{5... | collective-permute-start | bytes 1572872 | tf_op jit(solution)/shard_map/ppermute | solution.py:395
  372.2 19.0 %collective-permute-start.44 = (f32[256,512]{1,0:T(8,128)S(1)}, f32[256,512]{1,0:T(8,128)S(1)}, u32[]{:S(2)}, u32[]{:S(2)}) collective-permute-start(f32[256,512]{1,0:T(8,128)S(1)} %maximum_select_fusion.4), channel_id=1, source_target_pairs={{0,4},{4,0},{8,12},{12,8},{16,20},{20,16},{24,28},{28,24},{1,5},{5... | collective-permute-start | bytes 1572872 | tf_op jit(solution)/shard_map/ppermute | solution.py:395
  (71 other events, 648.7 us)
